TPU v7x, 256 devices: a whole 4x4x8 slice. The times are simulated.
256 devices in a mesh: blk: 32 (over z, y), rep: 8 (over x, core).
Axes of the slice: x: 4, y: 4, z: 8, core: 2. Of those that a mesh axis runs over, the one named last changes fastest.
Arguments:
- three_centre: bfloat16 [32, 7, 116, 29696], P('blk', None, None, 'rep'), may hold values from -0.21875 to 0.21875
- coeffs: bfloat16 [3712, 160], P('blk'), may hold values from -6 to 6
- neighbours: int32 [32, 7], P('blk'), may hold values from 0 to 31, as said below
- counts: int32 [32], P('blk'), may hold values from 1 to 7, as said below
Outputs:
- exchange_orbitals: float32 [3712, 160], P('blk', 'rep')
Inputs may be any that keep to these rules, and one draw needn't show every extreme that they name: `neighbours`: each row holds distinct molecules, the row's own molecule in slot 0. `counts`: in every draw some molecule uses all 7 slots.
All inputs are finite; a program needn't handle non-finite values.
Results may differ from a plain program's by a relative error of at most 0.0013.
Values may be sent and summed in bfloat16 or wider, within the bound.
A program may use at most 64 MiB of HBM per device.

v0:
```python
import math

import jax
import jax.numpy as jnp
from jax import lax
from jax.sharding import PartitionSpec as P


def shards(three_centre, coeffs, neighbours, counts):
    mol_dev, nlist, bs, width = three_centre.shape
    occ = coeffs.shape[1]
    blk_count = lax.axis_size("blk")
    rep_count = lax.axis_size("rep")
    total = bs * mol_dev * blk_count
    naux = width // bs
    aux_dev = naux // blk_count
    mscale = 1.0 / math.sqrt(total)
    oscale = 1.0 / math.sqrt(naux * rep_count * occ)
    gathered = lax.all_gather(coeffs, "blk", axis=0, tiled=True)
    blocks = gathered.reshape(total // bs, bs, occ)
    contract_first = (((0,), (0,)), ((), ()))
    used = (jnp.arange(nlist) < counts[0]).astype(jnp.bfloat16)
    picked = blocks[neighbours[0]] * used[:, None, None]
    left = three_centre[0].reshape(nlist * bs, width)
    product = lax.dot_general(
        left, picked.reshape(nlist * bs, occ), contract_first, preferred_element_type=jnp.float32
    )
    halves = [product.astype(jnp.bfloat16).reshape(naux, bs, occ)]
    stacked = jnp.stack(halves, axis=0)
    moved = jnp.transpose(stacked, (1, 0, 2, 3))
    moved = lax.all_to_all(moved, "blk", split_axis=0, concat_axis=1, tiled=True)
    spread = moved.reshape(aux_dev, total, occ)
    pairs = jnp.einsum("pni,nj->pij", spread, gathered, preferred_element_type=jnp.float32)
    pairs = (pairs * mscale).astype(jnp.bfloat16)
    mine = lax.psum_scatter(
        jnp.einsum("pni,pij->nj", spread, pairs, preferred_element_type=jnp.float32) * oscale,
        "blk",
        scatter_dimension=0,
        tiled=True,
    )
    return lax.psum_scatter(mine, "rep", scatter_dimension=1, tiled=True)


def solution(mesh):
    return jax.shard_map(
        shards,
        mesh=mesh,
        in_specs=(P("blk", None, None, "rep"), P("blk", None), P("blk", None), P("blk")),
        out_specs=P("blk", "rep"),
        check_vma=False,
    )
```

profile of v0, /device:TPU:1, one launch (start us, length us, event | category | flops | bytes accessed | tf_op | source)
XLA Modules:
  0.0 367.2 jit_solution(6083853292460890352)
XLA Ops:
  6.5 0.0 all-gather.3.cloned.1.call-start
  6.5 0.7 all-gather.3.cloned.1.call-update
  7.9 0.0 copy-start
  7.9 6.5 %reshape_squeeze.3 = bf16[812,3712]{1,0:T(8,128)(2,1)} reshape(bf16[1,7,116,3712]{3,2,1,0:T(8,128)(2,1)} %param.4) | data formatting | bytes 12056576 | tf_op jit(solution)/shard_map/reshape;squeeze | solution.py:24
  14.4 0.0 copy-done
  14.4 71.7 %all-gather.3.cloned.1.call-done = bf16[32,116,160]{1,2,0:T(8,128)(2,1)} async-done(((bf16[1,116,160]{1,2,0:T(8,128)(2,1)}), bf16[32,116,160]{1,2,0:T(8,128)(2,1)}) %all-gather.3.cloned.1.call-update) | async-done | bytes 1187856 | tf_op jit(solution)/shard_map/all_gather | solution.py:19
  86.1 1.9 gather_fusion
  88.0 0.1 broadcast_multiply_fusion
  88.1 0.1 copy.10
  88.3 0.2 mul.33
  88.5 4.2 %fusion = bf16[3712,160]{0,1:T(8,128)(2,1)S(1)} fusion(bf16[812,160]{0,1:T(8,128)(2,1)S(1)} %mul.33, bf16[812,3712]{1,0:T(8,128)(2,1)} %reshape_squeeze.3), kind=kOutput, calls=%fused_computation.3 | convolution fusion | flops 965120000 | bytes 7475968 | tf_op jit(solution)/shard_map/dot_general | solution.py:25
  92.7 5.3 %transpose_stack_reshape.3 = bf16[32,1,116,160]{2,0,3,1:T(8,128)(2,1)S(1)} reshape(bf16[3712,160]{0,1:T(8,128)(2,1)S(1)} %fusion) | data formatting | bytes 2375680 | tf_op jit(solution)/shard_map/transpose;stack;reshape | solution.py:30
  98.0 1.6 copy.11
  99.6 6.0 %all-to-all-start = ((bf16[32,1,116,160]{2,3,1,0:T(8,128)(2,1)}), bf16[32,1,116,160]{2,3,1,0:T(8,128)(2,1)S(1)}, u32[]{:S(2)}, u32[]{:S(2)}) async-start(bf16[32,1,116,160]{2,3,1,0:T(8,128)(2,1)} %copy.11), calls=%async_computation | async-start | bytes 2621440 | tf_op jit(solution)/shard_map/all_to_all | solution.py:31
  105.6 0.0 all-reduce.5.cloned.1.call-start
  105.6 1.8 copy.13
  107.4 3.0 reshape.96
  110.4 22.6 %all-to-all-done = bf16[32,1,116,160]{2,3,1,0:T(8,128)(2,1)S(1)} async-done(((bf16[32,1,116,160]{2,3,1,0:T(8,128)(2,1)}), bf16[32,1,116,160]{2,3,1,0:T(8,128)(2,1)S(1)}, u32[]{:S(2)}, u32[]{:S(2)}) %all-to-all-start) | async-done | bytes 1187872 | tf_op jit(solution)/shard_map/all_to_all | solution.py:31
  133.0 0.5 copy.12
  133.5 2.1 reshape.86
  135.7 4.3 %convolution_multiply_fusion = f32[3712,160]{0,1:T(8,128)} fusion(bf16[3712,160]{0,1:T(8,128)(2,1)S(1)} %reshape.86, bf16[3712,160]{0,1:T(8,128)(2,1)} %reshape.96), kind=kOutput, calls=%fused_computation.1 | convolution fusion | flops 380753920 | bytes 4751360 | tf_op jit(solution)/shard_map/pni,pij->nj/dot_general | solution.py:36
  140.0 0.0 copy-start.2
  140.0 0.0 copy-start.1
  140.0 0.0 all-reduce.5.cloned.1.call-update
  140.0 0.0 all-reduce.7.cloned.1.call-start
  140.1 0.6 copy-done.2
  140.7 0.6 dynamic-slice
  141.9 152.7 %all-reduce.5.cloned.1.call-done = f32[3712,160]{0,1:T(8,128)} async-done(((f32[3712,160]{0,1:T(8,128)}), f32[3712,160]{0,1:T(8,128)}) %all-reduce.5.cloned.1.call-update) | async-done | bytes 2375696
  294.6 1.6 constant_dynamic-slice_fusion.1
  296.2 0.0 all-reduce.7.cloned.1.call-update
  296.3 0.0 copy-done.1
  296.3 0.6 dynamic-slice.2
  297.5 61.8 %all-reduce.7.cloned.1.call-done = f32[116,160]{0,1:T(8,128)} async-done(((f32[116,160]{0,1:T(8,128)}), f32[116,160]{0,1:T(8,128)}) %all-reduce.7.cloned.1.call-update) | async-done | bytes 74256
  359.3 1.3 constant_dynamic-slice_fusion
  (3 shorter events, 0.0 us)
Async XLA Ops:
  6.5 79.6 %all-gather.3.cloned.1.call-start = ((), (), s32[]{:S(2)}) async-start(), calls=%async_computation.1 | async-start | bytes 1351680 | tf_op jit(solution)/shard_map/all_gather | solution.py:19
  7.9 6.5 %copy-start = (s32[1,7]{1,0:T(1,128)S(1)}, s32[1,7]{1,0:T(1,128)}, u32[]{:S(2)}) copy-start(s32[1,7]{1,0:T(1,128)} %param.6) | copy-start | bytes 88
  99.6 33.5 %all-to-all-start = ((bf16[32,1,116,160]{2,3,1,0:T(8,128)(2,1)}), bf16[32,1,116,160]{2,3,1,0:T(8,128)(2,1)S(1)}, u32[]{:S(2)}, u32[]{:S(2)}) async-start(bf16[32,1,116,160]{2,3,1,0:T(8,128)(2,1)} %copy.11), calls=%async_computation | async-start | bytes 2621440 | tf_op jit(solution)/shard_map/all_to_all | solution.py:31
  105.6 189.0 %all-reduce.5.cloned.1.call-start = ((), (), s32[]{:S(2)}) async-start(), calls=%async_computation.2 | async-start | bytes 4751360
  140.0 0.7 copy-start.2
  140.0 156.3 %copy-start.1 = (u32[256]{0:T(256)S(1)}, u32[256]{0:T(256)}, u32[]{:S(2)}) copy-start(u32[256]{0:T(256)} %constant.18) | copy-start | bytes 3076
  140.0 219.3 %all-reduce.7.cloned.1.call-start = ((), (), s32[]{:S(2)}) async-start(), calls=%async_computation.3 | async-start | bytes 163840
Sparse Core Ops, SparseCore 0:
  9.9 76.1 all-gather.2
  140.1 154.4 all-reduce.4
  297.0 62.2 all-reduce.6
where the time goes:
time: 368 us; the launch traced here: 367 us
  waiting for transfers between devices  310 us (84%)
  local copies, waits for them, and re-layouts  27.8 us (8%)
  between operations  15.2 us (4%)
  matrix products  8.44 us (2%)
  starting transfers between devices  6.06 us (2%)
    unnamed x5, waiting for transfers between devices  215 us
    all_gather x1, waiting for transfers between devices, shards(): gathered = lax.all_gather(coeffs, 'blk', axis=0, tiled=True)  71.7 us
    all_to_all x1, waiting for transfers between devices, shards(): lax.all_to_all(moved, 'blk', split_axis=0, concat_axis=1, tiled=True)  22.6 us
    unnamed x11, local copies, waits for them, and re-layouts  7.72 us
  transfers between devices with their start and end apart: 4, of which 4 were waited for; matrix products, arithmetic and copies ran while one was open for 3% of the time, Pallas kernels for 0%

commit v1 on v0

v1 whole, which is shorter than its diff:
```python
import functools
import math

import jax
import jax.numpy as jnp
from jax import lax
from jax.experimental import pallas as pl
from jax.experimental.pallas import tpu as pltpu
from jax.sharding import PartitionSpec as P

MESH = pl.DeviceIdType.MESH
NZ, NY, NX, NC = 8, 4, 4, 2
CHUNKS = ((0, 64), (64, 96))
BF16, F32 = jnp.bfloat16, jnp.float32


def kernel(
    t_ref, c_ref, nbr_ref, cnt_ref, o_ref,
    tv, tp, own, ct, ctp, pk, h, hs, hr, prf, prb, rsb, pf, oacc, frecv, fsum, f2,
    t_sem, s1s, s1r, s2s, s2r, cs, cr, a2s, a2r, rss, rsr, ags, agr, f1s, f1r, f2s, f2r,
):
    occ, bs = c_ref.shape
    nlist = t_ref.shape[1]
    width = t_ref.shape[3]
    naux = width // bs
    total = bs * NZ * NY
    mscale = 1.0 / math.sqrt(total)
    oscale = 1.0 / math.sqrt(naux * NX * NC * occ)
    blk, rep = lax.axis_index("blk"), lax.axis_index("rep")
    z, y, x, c = blk // NY, blk % NY, rep // NC, rep % NC
    zh, zl = z // 2, z % 2
    m_me = y * 2 + zl

    def dev(z_, y_, x_, c_):
        return (z_ * NY + y_, x_ * NC + c_)

    loads = [pltpu.make_async_copy(t_ref.at[0, l], tv.at[l], t_sem.at[l]) for l in range(nlist)]
    for load in loads:
        load.start()

    rel = [(dx, dy, dl) for dx in range(NX) for dy in range(NY) for dl in range(2)][1:]
    cls = x * NC + c
    self_here = cls == 0

    def s1_shift(dy):
        return lax.rem(cls + 2 * dy, NZ)

    def rel_dev(dx, dy, dl):
        return dev(zh * 2 + (zl + dl) % 2, (y + dy) % NY, (x + dx) % NX, c)

    sibling = dev(z, y, x, 1 - c)
    barrier = pltpu.get_barrier_semaphore()

    def hello(device):
        pl.semaphore_signal(barrier, inc=1, device_id=device, device_id_type=MESH)

    for r in rel:
        hello(rel_dev(*r))
    hello(sibling)
    for d in range(1, NZ // 2):
        hello(dev((z + 2 * d) % NZ, y, x, c))
    for dy in range(NY):
        source = dev((z + NZ - s1_shift(dy)) % NZ, (y + NY - dy) % NY, x, c)
        if dy == 0:
            pl.when(jnp.logical_not(self_here))(functools.partial(hello, source))
        else:
            hello(source)

    own[...] = jnp.concatenate([c_ref[...], jnp.zeros((occ, 128 - bs), BF16)], axis=1)

    count = len(rel) + 1 + (NZ // 2 - 1) + NY
    pl.semaphore_wait(barrier, jnp.where(self_here, count - 1, count))

    def s1_copy(ch, dy):
        r0, w = CHUNKS[ch]
        rows = pl.ds(r0, w)
        return pltpu.make_async_remote_copy(
            src_ref=own.at[rows, :], dst_ref=ct[ch].at[c, x, dy],
            send_sem=s1s.at[ch, dy], recv_sem=s1r.at[ch, dy],
            device_id=dev((z + s1_shift(dy)) % NZ, (y + dy) % NY, x, c), device_id_type=MESH,
        )

    def s1_local(ch):
        r0, w = CHUNKS[ch]
        rows = pl.ds(r0, w)
        return pltpu.make_async_copy(own.at[rows, :], ct[ch].at[c, x, 0], s1r.at[ch, 0])

    for ch in range(len(CHUNKS)):
        for dy in range(1, NY):
            s1_copy(ch, dy).start()
        pl.when(jnp.logical_not(self_here))(lambda ch=ch: s1_copy(ch, 0).start())
        pl.when(self_here)(lambda ch=ch: s1_local(ch).start())

    def s1_wait(ch):
        for dy in range(1, NY):
            s1_copy(ch, dy).wait_recv()
        pl.when(jnp.logical_not(self_here))(lambda: s1_copy(ch, 0).wait_recv())
        pl.when(self_here)(lambda: s1_local(ch).wait())

    def s2_copy(ch, d, x_src):
        part = ct[ch].at[c, x_src]
        return pltpu.make_async_remote_copy(
            src_ref=part, dst_ref=part, send_sem=s2s.at[ch, d - 1], recv_sem=s2r.at[ch, d - 1],
            device_id=dev(z, y, (x + d) % NX, c), device_id_type=MESH,
        )

    def core_copy(ch, c_src):
        part = ct[ch].at[c_src]
        return pltpu.make_async_remote_copy(
            src_ref=part, dst_ref=part, send_sem=cs.at[ch], recv_sem=cr.at[ch],
            device_id=sibling, device_id_type=MESH,
        )

    for l in range(nlist):
        loads[l].wait()
        top = bs // 16 * 16
        tp[l * 128 : l * 128 + top, :] = tv[l, 0:top, :]
        tail = tv[l, top:bs, :]
        tp[l * 128 + top : (l + 1) * 128, :] = jnp.concatenate(
            [tail, jnp.zeros((128 - bs, width), BF16)], axis=0
        )

    for ch in range(len(CHUNKS)):
        s1_wait(ch)
        for d in range(1, NX):
            s2_copy(ch, d, x).start()

    def place(b):
        zb, yb = b // NY, b % NY
        dy = (y + NY - yb) % NY
        s = (z + 2 * NZ - zb - 2 * dy) % NZ
        return s % NC, s // NC, dy

    def a2a_copy(ch, dy, dl, recv):
        w = CHUNKS[ch][1]
        y_, l_ = (y + dy) % NY, (zl + dl) % 2
        if recv:
            y_ = (y + NY - dy) % NY
            lanes = pl.ds(pl.multiple_of((y_ * 2 + l_) * 128, 128), 128)
        else:
            lanes = pl.ds(pl.multiple_of(m_me * 128, 128), 128)
        k = dy * 2 + dl
        return pltpu.make_async_remote_copy(
            src_ref=hs[ch].at[y_ * 2 + l_], dst_ref=hr[ch].at[:, lanes],
            send_sem=a2s.at[ch, k], recv_sem=a2r.at[ch, k],
            device_id=rel_dev(0, dy, dl), device_id_type=MESH,
        )

    def a2a_local(ch):
        lanes = pl.ds(pl.multiple_of(m_me * 128, 128), 128)
        return pltpu.make_async_copy(hs[ch].at[m_me], hr[ch].at[:, lanes], a2r.at[ch, 0])

    near = [(dy, dl) for dy in range(NY) for dl in range(2)][1:]

    for ch, (r0, w) in enumerate(CHUNKS):
        for d in range(1, NX):
            s2_copy(ch, d, (x + NX - d) % NX).wait_recv()
        core_copy(ch, c).start()
        core_copy(ch, 1 - c).wait_recv()
        for l in range(nlist):
            if l == 0:
                block = own[r0 : r0 + w, :]
            else:
                c_, x_, dy_ = place(nbr_ref[0, l])
                block = ct[ch][c_, x_, dy_]
            block = jnp.where(l < cnt_ref[0], block, jnp.zeros_like(block))
            pk[ch][:, l * 128 : (l + 1) * 128] = block
        for n0 in range(0, width, 512):
            n1 = min(n0 + 512, width)
            h[ch][:, n0:n1] = jnp.dot(
                pk[ch][...], tp[:, n0:n1], preferred_element_type=F32
            ).astype(BF16)
        for p in range(naux):
            lo = p * bs
            if lo + 128 <= width:
                piece = h[ch][:, lo : lo + 128]
            else:
                piece = jnp.concatenate(
                    [h[ch][:, lo:width], jnp.zeros((w, lo + 128 - width), BF16)], axis=1
                )
            hs[ch][p // 4, (p % 4) * w : (p % 4 + 1) * w, :] = piece
        for r in near:
            a2a_copy(ch, *r, False).start()
        a2a_local(ch).start()

    row = lax.broadcasted_iota(jnp.int32, (192, occ), 0)
    col = lax.broadcasted_iota(jnp.int32, (192, occ), 1)
    orbital = (row % 96 // 24 * NC + row // 96) * 20 + row % 24
    spread = jnp.logical_and(orbital == col, row % 24 < 20).astype(BF16)
    for y_ in range(NY):
        for l_ in range(2):
            m = y_ * 2 + l_
            c_, x_, dy_ = place((zh * 2 + l_) * NY + y_)
            ctp[:, m * 128 : (m + 1) * 128] = jnp.dot(
                spread,
                jnp.concatenate([part[c_, x_, dy_] for part in ct], axis=0),
                preferred_element_type=F32,
            ).astype(BF16)

    def rs_copy(ch, d):
        k = (zh + d) % 4
        return pltpu.make_async_remote_copy(
            src_ref=prb[ch].at[pl.ds(pl.multiple_of(k * 48, 16), 48), :], dst_ref=rsb[ch].at[d - 1],
            send_sem=rss.at[ch, d - 1], recv_sem=rsr.at[ch, d - 1],
            device_id=dev((z + 2 * d) % NZ, y, x, c), device_id_type=MESH,
        )

    def ag_copy(ch, d, k):
        part = pf[ch].at[pl.ds(pl.multiple_of(k * 48, 16), 48), :]
        return pltpu.make_async_remote_copy(
            src_ref=part, dst_ref=part,
            send_sem=ags.at[ch, d - 1], recv_sem=agr.at[ch, d - 1],
            device_id=dev((z + 2 * d) % NZ, y, x, c), device_id_type=MESH,
        )

    for ch in range(len(CHUNKS)):
        a2a_local(ch).wait()
        for r in near:
            a2a_copy(ch, *r, True).wait_recv()
        part = lax.dot_general(
            ctp[...], hr[ch][...], (((1,), (1,)), ((), ())), preferred_element_type=F32
        )
        prf[ch][...] = part
        prb[ch][...] = part.astype(BF16)
        for d in range(1, 4):
            rs_copy(ch, d).start()

    mine = pl.ds(pl.multiple_of(zh * 48, 16), 48)
    for ch in range(len(CHUNKS)):
        for d in range(1, 4):
            rs_copy(ch, d).wait_recv()
        whole = prf[ch][mine, :]
        for d in range(1, 4):
            whole = whole + rsb[ch][d - 1].astype(F32)
        pf[ch][mine, :] = (whole * mscale).astype(BF16)
        for d in range(1, 4):
            ag_copy(ch, d, zh).start()

    for ch in range(len(CHUNKS)):
        for d in range(1, 4):
            ag_copy(ch, d, (zh + 4 - d) % 4).wait_recv()
        part = jnp.dot(pf[ch][...], hr[ch][...], preferred_element_type=F32)
        if ch == 0:
            oacc[...] = part
        else:
            oacc[...] += part

    f1 = pltpu.make_async_remote_copy(
        src_ref=oacc.at[pl.ds(pl.multiple_of((1 - c) * 96, 8), 96), :], dst_ref=frecv,
        send_sem=f1s, recv_sem=f1r, device_id=sibling, device_id_type=MESH,
    )
    f1.start()
    f1.wait_recv()
    fsum[...] = oacc[pl.ds(pl.multiple_of(c * 96, 8), 96), :] + frecv[...]

    def f2_copy(i):
        dx, dy, dl = rel[i]
        x_, y_, l_ = (x + dx) % NX, (y + dy) % NY, (zl + dl) % 2
        return pltpu.make_async_remote_copy(
            src_ref=fsum.at[
                pl.ds(pl.multiple_of(x_ * 24, 8), 24),
                pl.ds(pl.multiple_of((y_ * 2 + l_) * 128, 128), 128),
            ],
            dst_ref=f2.at[i], send_sem=f2s.at[i], recv_sem=f2r.at[i],
            device_id=rel_dev(dx, dy, dl), device_id_type=MESH,
        )

    for i in range(len(rel)):
        f2_copy(i).start()
    done = fsum[
        pl.ds(pl.multiple_of(x * 24, 8), 24), pl.ds(pl.multiple_of(m_me * 128, 128), 128)
    ]
    for i in range(len(rel)):
        f2_copy(i).wait_recv()
        done = done + f2[i]
    o_ref[...] = (done * oscale)[:20, :bs]

    for ch in range(len(CHUNKS)):
        for dy in range(1, NY):
            s1_copy(ch, dy).wait_send()
        pl.when(jnp.logical_not(self_here))(lambda ch=ch: s1_copy(ch, 0).wait_send())
        for d in range(1, NX):
            s2_copy(ch, d, x).wait_send()
        core_copy(ch, c).wait_send()
        for r in near:
            a2a_copy(ch, *r, False).wait_send()
        for d in range(1, 4):
            rs_copy(ch, d).wait_send()
            ag_copy(ch, d, zh).wait_send()
    f1.wait_send()
    for i in range(len(rel)):
        f2_copy(i).wait_send()


def shards(three_centre, coeffs, neighbours, counts):
    _, nlist, bs, width = three_centre.shape
    occ = coeffs.shape[1]
    n = len(CHUNKS)
    ws = [w for _, w in CHUNKS]
    dma = pltpu.SemaphoreType.DMA
    scratch = [
        pltpu.VMEM((nlist, bs, width), BF16),
        pltpu.VMEM((nlist * 128, width), BF16),
        pltpu.VMEM((occ, 128), BF16),
        [pltpu.VMEM((NC, NX, NY, w, 128), BF16) for w in ws],
        pltpu.VMEM((192, 1024), BF16),
        [pltpu.VMEM((w, nlist * 128), BF16) for w in ws],
        [pltpu.VMEM((w, width), BF16) for w in ws],
        [pltpu.VMEM((8, 4 * w, 128), BF16) for w in ws],
        [pltpu.VMEM((4 * w, 1024), BF16) for w in ws],
        [pltpu.VMEM((192, 4 * w), F32) for w in ws],
        [pltpu.VMEM((192, 4 * w), BF16) for w in ws],
        [pltpu.VMEM((3, 48, 4 * w), BF16) for w in ws],
        [pltpu.VMEM((192, 4 * w), BF16) for w in ws],
        pltpu.VMEM((192, 1024), F32),
        pltpu.VMEM((96, 1024), F32),
        pltpu.VMEM((96, 1024), F32),
        pltpu.VMEM((31, 24, 128), F32),
        dma((nlist,)),
        dma((n, NY)), dma((n, NY)),
        dma((n, 3)), dma((n, 3)),
        dma((n,)), dma((n,)),
        dma((n, 8)), dma((n, 8)),
        dma((n, 3)), dma((n, 3)),
        dma((n, 3)), dma((n, 3)),
        dma, dma,
        dma((31,)), dma((31,)),
    ]
    return pl.pallas_call(
        kernel,
        out_shape=jax.ShapeDtypeStruct((occ // (NX * NC), bs), F32),
        in_specs=[
            pl.BlockSpec(memory_space=pl.ANY),
            pl.BlockSpec(memory_space=pltpu.VMEM),
            pl.BlockSpec(memory_space=pltpu.SMEM),
            pl.BlockSpec(memory_space=pltpu.SMEM),
        ],
        out_specs=pl.BlockSpec(memory_space=pltpu.VMEM),
        scratch_shapes=scratch,
        compiler_params=pltpu.CompilerParams(
            collective_id=0, has_side_effects=True, vmem_limit_bytes=48 * 2**20
        ),
    )(three_centre, coeffs.T, neighbours, counts).T


def solution(mesh):
    return jax.shard_map(
        shards,
        mesh=mesh,
        in_specs=(P("blk", None, None, "rep"), P("blk", None), P("blk", None), P("blk")),
        out_specs=P("blk", "rep"),
        check_vma=False,
    )
```

time: 368 us -> 69.4 us (0.19)
  waiting for transfers between devices: 310 us -> 0 us
  Pallas kernels: 0 us -> 66.6 us
  local copies, waits for them, and re-layouts: 27.8 us -> 2.03 us
  between operations: 15.2 us -> 0.67 us
  matrix products: 8.44 us -> 0 us
  starting transfers between devices: 6.06 us -> 0 us
    unnamed x5 -> x0, waiting for transfers between devices: 215 us -> none
    all_gather x1 -> x0, waiting for transfers between devices: 71.7 us -> none  [shards(): gathered = lax.all_gather(coeffs, 'blk', axis=0, tiled=True)]
    pallas_call x0 -> x1, Pallas kernels: none -> 66.6 us  [shards(): pl.pallas_call(kernel, out_shape=jax.ShapeDtypeStruct((occ // (NX * NC),...]
    all_to_all x1 -> x0, waiting for transfers between devices: 22.6 us -> none  [shards(): lax.all_to_all(moved, 'blk', split_axis=0, concat_axis=1, tiled=True)]
    another operation x4 -> x0, local copies, waits for them, and re-layouts: 15.5 us -> none  [the longest x2 6.87 us: shards(): moved = jnp.transpose(stacked, (1, 0, 2, 3))]
    dot_general x2 -> x0, matrix products: 8.44 us -> none  [the longest x1 4.29 us: shards(): jnp.einsum('pni,pij->nj', spread, pairs, preferred_element_type=jnp.float32)]
    all_to_all x1 -> x0, starting transfers between devices: 5.98 us -> none  [shards(): lax.all_to_all(moved, 'blk', split_axis=0, concat_axis=1, tiled=True)]
    unnamed x11 -> x5, local copies, waits for them, and re-layouts: 7.72 us -> 2.03 us
  transfers between devices with their start and end apart: 4 -> 0, of which waited for: 4 -> 0; matrix products, arithmetic and copies ran while one was open for 3% -> 0% of each run, Pallas kernels for 0% -> 0%
where the time goes in v1:
time: 69.4 us; the launch traced here: 69.3 us
  Pallas kernels  66.6 us (96%)
  local copies, waits for them, and re-layouts  2.03 us (3%)
    pallas_call x1, Pallas kernels, shards(): pl.pallas_call(kernel, out_shape=jax.ShapeDtypeStruct((occ // (NX * NC),...  66.6 us
    unnamed x5, local copies, waits for them, and re-layouts  2.03 us

profile of v1, /device:TPU:1, one launch (start us, length us, event | category | flops | bytes accessed | tf_op | source)
XLA Modules:
  0.0 69.3 jit_solution(15131595379211504722)
XLA Ops:
  0.7 0.0 copy-start
  0.7 0.8 %copy-done = bf16[116,160]{0,1:T(8,128)(2,1)S(1)} copy-done((bf16[116,160]{0,1:T(8,128)(2,1)S(1)}, bf16[116,160]{0,1:T(8,128)(2,1)}, u32[]{:S(2)}) %copy-start) | copy-done | bytes 37144
  1.4 0.0 copy-start.1
  1.4 0.7 copy-done.1
  2.1 66.6 %shard_map.46 = f32[20,116]{1,0:T(8,128)S(1)} custom-call(bf16[1,7,116,3712]{3,2,1,0:T(8,128)(2,1)} %t_ref.1, bf16[160,116]{1,0:T(8,128)(2,1)S(1)} %bitcast.3, s32[1,7]{1,0:T(1,128)S(1)} %copy-done.1, s32[1]{0:T(128)S(6)} %copy.6.cnt_ref), custom_call_target="tpu_custom_call" | custom-call | tf_op jit(solution)/shard_map/pallas_call | solution.py:329
  68.7 0.6 copy.7
Async XLA Ops:
  0.7 0.8 %copy-start = (bf16[116,160]{0,1:T(8,128)(2,1)S(1)}, bf16[116,160]{0,1:T(8,128)(2,1)}, u32[]{:S(2)}) copy-start(bf16[116,160]{0,1:T(8,128)(2,1)} %param.5) | copy-start | bytes 111364
  1.4 0.7 copy-start.1

commit v2 on v1

--- a/solution.py
+++ b/solution.py
@@ -10,14 +10,14 @@
 
 MESH = pl.DeviceIdType.MESH
 NZ, NY, NX, NC = 8, 4, 4, 2
-CHUNKS = ((0, 64), (64, 96))
+CHUNKS = ((0, 32), (32, 64), (96, 64))
 BF16, F32 = jnp.bfloat16, jnp.float32
 
 
 def kernel(
-    t_ref, c_ref, nbr_ref, cnt_ref, o_ref,
-    tv, tp, own, ct, ctp, pk, h, hs, hr, prf, prb, rsb, pf, oacc, frecv, fsum, f2,
-    t_sem, s1s, s1r, s2s, s2r, cs, cr, a2s, a2r, rss, rsr, ags, agr, f1s, f1r, f2s, f2r,
+    t_ref, c_hbm, nbr_hbm, cnt_hbm, o_ref,
+    c_ref, nbr_ref, cnt_ref, tv, tp, own, ct, ctp, pk, h, hs, hr, prf, prb, rsb, pf, oacc, frecv, fsum, fb, f2,
+    t_sem, in_sem, s1s, s1r, s2s, s2r, cs, cr, a2s, a2r, rss, rsr, ags, agr, f1s, f1r, f2s, f2r,
 ):
     occ, bs = c_ref.shape
     nlist = t_ref.shape[1]
@@ -34,11 +34,38 @@
     def dev(z_, y_, x_, c_):
         return (z_ * NY + y_, x_ * NC + c_)
 
+    small = [
+        pltpu.make_async_copy(src, dst, in_sem.at[i])
+        for i, (src, dst) in enumerate(((c_hbm, c_ref), (nbr_hbm, nbr_ref), (cnt_hbm, cnt_ref)))
+    ]
+    for load in small:
+        load.start()
     loads = [pltpu.make_async_copy(t_ref.at[0, l], tv.at[l], t_sem.at[l]) for l in range(nlist)]
     for load in loads:
         load.start()
 
+    sent = []
+
+    def send(copy, when=None):
+        def start():
+            copy().start()
+
+        def wait():
+            copy().wait_send()
+
+        if when is None:
+            start()
+            sent.append(wait)
+        else:
+            pl.when(when)(start)
+            sent.append(lambda: pl.when(when)(wait))
+
+    def finish():
+        while sent:
+            sent.pop(0)()
+
     rel = [(dx, dy, dl) for dx in range(NX) for dy in range(NY) for dl in range(2)][1:]
+    rel.sort(key=lambda r: min(r[0], NX - r[0]) + min(r[1], NY - r[1]) + r[2])
     cls = x * NC + c
     self_here = cls == 0
 
@@ -66,6 +93,8 @@
         else:
             hello(source)
 
+    for load in small:
+        load.wait()
     own[...] = jnp.concatenate([c_ref[...], jnp.zeros((occ, 128 - bs), BF16)], axis=1)
 
     count = len(rel) + 1 + (NZ // 2 - 1) + NY
@@ -73,22 +102,20 @@
 
     def s1_copy(ch, dy):
         r0, w = CHUNKS[ch]
-        rows = pl.ds(r0, w)
-        return pltpu.make_async_remote_copy(
-            src_ref=own.at[rows, :], dst_ref=ct[ch].at[c, x, dy],
+        return pltpu.make_async_remote_copy(
+            src_ref=own.at[pl.ds(r0, w), :], dst_ref=ct[ch].at[c, x, dy],
             send_sem=s1s.at[ch, dy], recv_sem=s1r.at[ch, dy],
             device_id=dev((z + s1_shift(dy)) % NZ, (y + dy) % NY, x, c), device_id_type=MESH,
         )
 
     def s1_local(ch):
         r0, w = CHUNKS[ch]
-        rows = pl.ds(r0, w)
-        return pltpu.make_async_copy(own.at[rows, :], ct[ch].at[c, x, 0], s1r.at[ch, 0])
-
-    for ch in range(len(CHUNKS)):
-        for dy in range(1, NY):
-            s1_copy(ch, dy).start()
-        pl.when(jnp.logical_not(self_here))(lambda ch=ch: s1_copy(ch, 0).start())
+        return pltpu.make_async_copy(own.at[pl.ds(r0, w), :], ct[ch].at[c, x, 0], s1r.at[ch, 0])
+
+    for ch in range(len(CHUNKS)):
+        for dy in (2, 1, 3):
+            send(functools.partial(s1_copy, ch, dy))
+        send(functools.partial(s1_copy, ch, 0), jnp.logical_not(self_here))
         pl.when(self_here)(lambda ch=ch: s1_local(ch).start())
 
     def s1_wait(ch):
@@ -122,8 +149,8 @@
 
     for ch in range(len(CHUNKS)):
         s1_wait(ch)
-        for d in range(1, NX):
-            s2_copy(ch, d, x).start()
+        for d in (2, 1, 3):
+            send(functools.partial(s2_copy, ch, d, x))
 
     def place(b):
         zb, yb = b // NY, b % NY
@@ -131,31 +158,22 @@
         s = (z + 2 * NZ - zb - 2 * dy) % NZ
         return s % NC, s // NC, dy
 
-    def a2a_copy(ch, dy, dl, recv):
-        w = CHUNKS[ch][1]
-        y_, l_ = (y + dy) % NY, (zl + dl) % 2
-        if recv:
-            y_ = (y + NY - dy) % NY
-            lanes = pl.ds(pl.multiple_of((y_ * 2 + l_) * 128, 128), 128)
-        else:
-            lanes = pl.ds(pl.multiple_of(m_me * 128, 128), 128)
-        k = dy * 2 + dl
-        return pltpu.make_async_remote_copy(
-            src_ref=hs[ch].at[y_ * 2 + l_], dst_ref=hr[ch].at[:, lanes],
-            send_sem=a2s.at[ch, k], recv_sem=a2r.at[ch, k],
-            device_id=rel_dev(0, dy, dl), device_id_type=MESH,
-        )
-
-    def a2a_local(ch):
-        lanes = pl.ds(pl.multiple_of(m_me * 128, 128), 128)
-        return pltpu.make_async_copy(hs[ch].at[m_me], hr[ch].at[:, lanes], a2r.at[ch, 0])
-
-    near = [(dy, dl) for dy in range(NY) for dl in range(2)][1:]
+    def a2a_copy(ch, to, source):
+        lanes = pl.ds(pl.multiple_of(source * 128, 128), 128)
+        return pltpu.make_async_remote_copy(
+            src_ref=hs[ch].at[to], dst_ref=hr[ch].at[:, lanes],
+            send_sem=a2s.at[ch, to], recv_sem=a2r.at[ch, source],
+            device_id=dev(zh * 2 + to % 2, to // 2, x, c), device_id_type=MESH,
+        )
+
+    def a2a_local(ch, m):
+        lanes = pl.ds(m * 128, 128)
+        return pltpu.make_async_copy(hs[ch].at[m], hr[ch].at[:, lanes], a2r.at[ch, m])
 
     for ch, (r0, w) in enumerate(CHUNKS):
         for d in range(1, NX):
             s2_copy(ch, d, (x + NX - d) % NX).wait_recv()
-        core_copy(ch, c).start()
+        send(functools.partial(core_copy, ch, c))
         core_copy(ch, 1 - c).wait_recv()
         for l in range(nlist):
             if l == 0:
@@ -165,23 +183,22 @@
                 block = ct[ch][c_, x_, dy_]
             block = jnp.where(l < cnt_ref[0], block, jnp.zeros_like(block))
             pk[ch][:, l * 128 : (l + 1) * 128] = block
-        for n0 in range(0, width, 512):
-            n1 = min(n0 + 512, width)
+        for m in range(8):
+            n0, n1 = m * 512, min((m + 1) * 512, width)
             h[ch][:, n0:n1] = jnp.dot(
                 pk[ch][...], tp[:, n0:n1], preferred_element_type=F32
             ).astype(BF16)
-        for p in range(naux):
-            lo = p * bs
-            if lo + 128 <= width:
-                piece = h[ch][:, lo : lo + 128]
-            else:
-                piece = jnp.concatenate(
-                    [h[ch][:, lo:width], jnp.zeros((w, lo + 128 - width), BF16)], axis=1
-                )
-            hs[ch][p // 4, (p % 4) * w : (p % 4 + 1) * w, :] = piece
-        for r in near:
-            a2a_copy(ch, *r, False).start()
-        a2a_local(ch).start()
+            for k in range(4):
+                lo = (m * 4 + k) * bs
+                if lo + 128 <= width:
+                    piece = h[ch][:, lo : lo + 128]
+                else:
+                    piece = jnp.concatenate(
+                        [h[ch][:, lo:width], jnp.zeros((w, lo + 128 - width), BF16)], axis=1
+                    )
+                hs[ch][m, k * w : (k + 1) * w, :] = piece
+            send(functools.partial(a2a_copy, ch, m, m_me), m != m_me)
+            pl.when(m == m_me)(lambda m=m: a2a_local(ch, m).start())
 
     row = lax.broadcasted_iota(jnp.int32, (192, occ), 0)
     col = lax.broadcasted_iota(jnp.int32, (192, occ), 1)
@@ -214,17 +231,18 @@
         )
 
     for ch in range(len(CHUNKS)):
-        a2a_local(ch).wait()
-        for r in near:
-            a2a_copy(ch, *r, True).wait_recv()
+        for m in range(8):
+            pl.when(m != m_me)(lambda m=m: a2a_copy(ch, m, m).wait_recv())
+            pl.when(m == m_me)(lambda m=m: a2a_local(ch, m).wait())
         part = lax.dot_general(
             ctp[...], hr[ch][...], (((1,), (1,)), ((), ())), preferred_element_type=F32
         )
         prf[ch][...] = part
         prb[ch][...] = part.astype(BF16)
         for d in range(1, 4):
-            rs_copy(ch, d).start()
-
+            send(functools.partial(rs_copy, ch, d))
+
+    finish()
     mine = pl.ds(pl.multiple_of(zh * 48, 16), 48)
     for ch in range(len(CHUNKS)):
         for d in range(1, 4):
@@ -234,7 +252,7 @@
             whole = whole + rsb[ch][d - 1].astype(F32)
         pf[ch][mine, :] = (whole * mscale).astype(BF16)
         for d in range(1, 4):
-            ag_copy(ch, d, zh).start()
+            send(functools.partial(ag_copy, ch, d, zh))
 
     for ch in range(len(CHUNKS)):
         for d in range(1, 4):
@@ -249,47 +267,33 @@
         src_ref=oacc.at[pl.ds(pl.multiple_of((1 - c) * 96, 8), 96), :], dst_ref=frecv,
         send_sem=f1s, recv_sem=f1r, device_id=sibling, device_id_type=MESH,
     )
-    f1.start()
+    send(lambda: f1)
     f1.wait_recv()
     fsum[...] = oacc[pl.ds(pl.multiple_of(c * 96, 8), 96), :] + frecv[...]
+
+    for x_ in range(NX):
+        rows = [fsum[x_ * 24 : (x_ + 1) * 24, :], jnp.zeros((8, 1024), F32)]
+        fb[x_] = jnp.concatenate(rows, axis=0).astype(BF16)
 
     def f2_copy(i):
         dx, dy, dl = rel[i]
         x_, y_, l_ = (x + dx) % NX, (y + dy) % NY, (zl + dl) % 2
         return pltpu.make_async_remote_copy(
-            src_ref=fsum.at[
-                pl.ds(pl.multiple_of(x_ * 24, 8), 24),
-                pl.ds(pl.multiple_of((y_ * 2 + l_) * 128, 128), 128),
-            ],
+            src_ref=fb.at[x_, :, pl.ds(pl.multiple_of((y_ * 2 + l_) * 128, 128), 128)],
             dst_ref=f2.at[i], send_sem=f2s.at[i], recv_sem=f2r.at[i],
             device_id=rel_dev(dx, dy, dl), device_id_type=MESH,
         )
 
-    for i in range(len(rel)):
-        f2_copy(i).start()
+    for i in reversed(range(len(rel))):
+        send(functools.partial(f2_copy, i))
+    finish()
     done = fsum[
         pl.ds(pl.multiple_of(x * 24, 8), 24), pl.ds(pl.multiple_of(m_me * 128, 128), 128)
     ]
     for i in range(len(rel)):
         f2_copy(i).wait_recv()
-        done = done + f2[i]
+        done = done + f2[i].astype(F32)[:24]
     o_ref[...] = (done * oscale)[:20, :bs]
-
-    for ch in range(len(CHUNKS)):
-        for dy in range(1, NY):
-            s1_copy(ch, dy).wait_send()
-        pl.when(jnp.logical_not(self_here))(lambda ch=ch: s1_copy(ch, 0).wait_send())
-        for d in range(1, NX):
-            s2_copy(ch, d, x).wait_send()
-        core_copy(ch, c).wait_send()
-        for r in near:
-            a2a_copy(ch, *r, False).wait_send()
-        for d in range(1, 4):
-            rs_copy(ch, d).wait_send()
-            ag_copy(ch, d, zh).wait_send()
-    f1.wait_send()
-    for i in range(len(rel)):
-        f2_copy(i).wait_send()
 
 
 def shards(three_centre, coeffs, neighbours, counts):
@@ -299,6 +303,9 @@
     ws = [w for _, w in CHUNKS]
     dma = pltpu.SemaphoreType.DMA
     scratch = [
+        pltpu.VMEM((occ, bs), BF16),
+        pltpu.SMEM((1, nlist), jnp.int32),
+        pltpu.SMEM((1,), jnp.int32),
         pltpu.VMEM((nlist, bs, width), BF16),
         pltpu.VMEM((nlist * 128, width), BF16),
         pltpu.VMEM((occ, 128), BF16),
@@ -315,8 +322,10 @@
         pltpu.VMEM((192, 1024), F32),
         pltpu.VMEM((96, 1024), F32),
         pltpu.VMEM((96, 1024), F32),
-        pltpu.VMEM((31, 24, 128), F32),
+        pltpu.VMEM((NX, 32, 1024), BF16),
+        pltpu.VMEM((31, 32, 128), BF16),
         dma((nlist,)),
+        dma((3,)),
         dma((n, NY)), dma((n, NY)),
         dma((n, 3)), dma((n, 3)),
         dma((n,)), dma((n,)),
@@ -331,14 +340,14 @@
         out_shape=jax.ShapeDtypeStruct((occ // (NX * NC), bs), F32),
         in_specs=[
             pl.BlockSpec(memory_space=pl.ANY),
-            pl.BlockSpec(memory_space=pltpu.VMEM),
-            pl.BlockSpec(memory_space=pltpu.SMEM),
-            pl.BlockSpec(memory_space=pltpu.SMEM),
+            pl.BlockSpec(memory_space=pl.ANY),
+            pl.BlockSpec(memory_space=pl.ANY),
+            pl.BlockSpec(memory_space=pl.ANY),
         ],
         out_specs=pl.BlockSpec(memory_space=pltpu.VMEM),
         scratch_shapes=scratch,
         compiler_params=pltpu.CompilerParams(
-            collective_id=0, has_side_effects=True, vmem_limit_bytes=48 * 2**20
+            collective_id=0, has_side_effects=True, vmem_limit_bytes=60 * 2**20
         ),
     )(three_centre, coeffs.T, neighbours, counts).T
 

time: 69.4 us -> 66.1 us (0.952)
  Pallas kernels: 66.6 us -> 64 us
  local copies, waits for them, and re-layouts: 2.03 us -> 1.31 us
    pallas_call x1, Pallas kernels: 66.6 us -> 64 us  [shards(): pl.pallas_call(kernel, out_shape=jax.ShapeDtypeStruct((occ // (NX * NC),...]
    unnamed x5 -> x1, local copies, waits for them, and re-layouts: 2.03 us -> 1.31 us
where the time goes in v2:
time: 66.1 us; the launch traced here: 65.9 us
  Pallas kernels  64 us (97%)
  local copies, waits for them, and re-layouts  1.31 us (2%)
    pallas_call x1, Pallas kernels, shards(): pl.pallas_call(kernel, out_shape=jax.ShapeDtypeStruct((occ // (NX * NC),...  64 us

profile of v2, /device:TPU:1, one launch (start us, length us, event | category | flops | bytes accessed | tf_op | source)
XLA Modules:
  0.0 65.9 jit_solution(7731306137287187165)
XLA Ops:
  0.7 64.0 %shard_map.46 = f32[20,116]{1,0:T(8,128)} custom-call(bf16[1,7,116,3712]{3,2,1,0:T(8,128)(2,1)} %t_ref.1, bf16[160,116]{1,0:T(8,128)(2,1)} %bitcast.3, s32[1,7]{1,0:T(1,128)} %nbr_hbm.1, s32[1]{0:T(128)S(6)} %copy.6.cnt_hbm), custom_call_target="tpu_custom_call" | custom-call | tf_op jit(solution)/shard_map/pallas_call | solution.py:338
  64.6 1.3 %copy.7 = f32[116,20]{0,1:T(8,128)} copy(f32[116,20]{0,1:T(8,128)} %bitcast.2) | data formatting | bytes 18560

commit v3 on v2

--- a/solution.py
+++ b/solution.py
@@ -11,12 +11,14 @@
 MESH = pl.DeviceIdType.MESH
 NZ, NY, NX, NC = 8, 4, 4, 2
 CHUNKS = ((0, 32), (32, 64), (96, 64))
+ORDER = ("h0", "h1", "h2", "c", "a0", "a1", "r0", "a2", "r1", "r2", "f", "g0", "g1", "g2")
+EARLY = 5
 BF16, F32 = jnp.bfloat16, jnp.float32
 
 
 def kernel(
     t_ref, c_hbm, nbr_hbm, cnt_hbm, o_ref,
-    c_ref, nbr_ref, cnt_ref, tv, tp, own, ct, ctp, pk, h, hs, hr, prf, prb, rsb, pf, oacc, frecv, fsum, fb, f2,
+    c_ref, nbr_ref, cnt_ref, tv, tp, own, ct, ctp, pk, h, hs, hr, prf, prb, rsb, pf, oacc, fa, frecv, fb, ff, f2,
     t_sem, in_sem, s1s, s1r, s2s, s2r, cs, cr, a2s, a2r, rss, rsr, ags, agr, f1s, f1r, f2s, f2r,
 ):
     occ, bs = c_ref.shape
@@ -28,8 +30,6 @@
     oscale = 1.0 / math.sqrt(naux * NX * NC * occ)
     blk, rep = lax.axis_index("blk"), lax.axis_index("rep")
     z, y, x, c = blk // NY, blk % NY, rep // NC, rep % NC
-    zh, zl = z // 2, z % 2
-    m_me = y * 2 + zl
 
     def dev(z_, y_, x_, c_):
         return (z_ * NY + y_, x_ * NC + c_)
@@ -64,16 +64,17 @@
         while sent:
             sent.pop(0)()
 
-    rel = [(dx, dy, dl) for dx in range(NX) for dy in range(NY) for dl in range(2)][1:]
-    rel.sort(key=lambda r: min(r[0], NX - r[0]) + min(r[1], NY - r[1]) + r[2])
+    rel = [(dx, dy) for dx in range(NX) for dy in range(NY)][1:]
+    rel.sort(key=lambda r: min(r[0], NX - r[0]) + min(r[1], NY - r[1]))
+    around = (4, 3, 5, 2, 6, 1, 7)
     cls = x * NC + c
     self_here = cls == 0
 
     def s1_shift(dy):
         return lax.rem(cls + 2 * dy, NZ)
 
-    def rel_dev(dx, dy, dl):
-        return dev(zh * 2 + (zl + dl) % 2, (y + dy) % NY, (x + dx) % NX, c)
+    def rel_dev(dx, dy):
+        return dev(z, (y + dy) % NY, (x + dx) % NX, c)
 
     sibling = dev(z, y, x, 1 - c)
     barrier = pltpu.get_barrier_semaphore()
@@ -84,8 +85,8 @@
     for r in rel:
         hello(rel_dev(*r))
     hello(sibling)
-    for d in range(1, NZ // 2):
-        hello(dev((z + 2 * d) % NZ, y, x, c))
+    for d in around:
+        hello(dev((z + d) % NZ, y, x, c))
     for dy in range(NY):
         source = dev((z + NZ - s1_shift(dy)) % NZ, (y + NY - dy) % NY, x, c)
         if dy == 0:
@@ -97,7 +98,7 @@
         load.wait()
     own[...] = jnp.concatenate([c_ref[...], jnp.zeros((occ, 128 - bs), BF16)], axis=1)
 
-    count = len(rel) + 1 + (NZ // 2 - 1) + NY
+    count = len(rel) + 1 + len(around) + NY
     pl.semaphore_wait(barrier, jnp.where(self_here, count - 1, count))
 
     def s1_copy(ch, dy):
@@ -163,17 +164,22 @@
         return pltpu.make_async_remote_copy(
             src_ref=hs[ch].at[to], dst_ref=hr[ch].at[:, lanes],
             send_sem=a2s.at[ch, to], recv_sem=a2r.at[ch, source],
-            device_id=dev(zh * 2 + to % 2, to // 2, x, c), device_id_type=MESH,
+            device_id=dev(z, to, x, c), device_id_type=MESH,
         )
 
     def a2a_local(ch, m):
         lanes = pl.ds(m * 128, 128)
         return pltpu.make_async_copy(hs[ch].at[m], hr[ch].at[:, lanes], a2r.at[ch, m])
 
-    for ch, (r0, w) in enumerate(CHUNKS):
+    def to_sibling(ch):
         for d in range(1, NX):
             s2_copy(ch, d, (x + NX - d) % NX).wait_recv()
         send(functools.partial(core_copy, ch, c))
+
+    def halves(ch):
+        r0, w = CHUNKS[ch]
+        if ch == 0:
+            to_sibling(0)
         core_copy(ch, 1 - c).wait_recv()
         for l in range(nlist):
             if l == 0:
@@ -196,104 +202,152 @@
                     piece = jnp.concatenate(
                         [h[ch][:, lo:width], jnp.zeros((w, lo + 128 - width), BF16)], axis=1
                     )
-                hs[ch][m, k * w : (k + 1) * w, :] = piece
-            send(functools.partial(a2a_copy, ch, m, m_me), m != m_me)
-            pl.when(m == m_me)(lambda m=m: a2a_local(ch, m).start())
-
-    row = lax.broadcasted_iota(jnp.int32, (192, occ), 0)
-    col = lax.broadcasted_iota(jnp.int32, (192, occ), 1)
-    orbital = (row % 96 // 24 * NC + row // 96) * 20 + row % 24
-    spread = jnp.logical_and(orbital == col, row % 24 < 20).astype(BF16)
-    for y_ in range(NY):
-        for l_ in range(2):
-            m = y_ * 2 + l_
-            c_, x_, dy_ = place((zh * 2 + l_) * NY + y_)
-            ctp[:, m * 128 : (m + 1) * 128] = jnp.dot(
+                r0 = (m % 2 * 4 + k) * w
+                hs[ch][m // 2, r0 : r0 + w, :] = piece
+            if m % 2:
+                to = m // 2
+                send(functools.partial(a2a_copy, ch, to, y), to != y)
+                pl.when(to == y)(lambda to=to: a2a_local(ch, to).start())
+            if m == EARLY and ch + 1 < len(CHUNKS):
+                to_sibling(ch + 1)
+
+    def group():
+        row = lax.broadcasted_iota(jnp.int32, (256, occ), 0)
+        col = lax.broadcasted_iota(jnp.int32, (256, occ), 1)
+        first = (row % 64 // 16 * NC + row // 64) * 20 + row % 16
+        last = (row % 16 // 4 * NC + row % 32 // 16) * 20 + 16 + row % 4
+        spread = (jnp.where(row < 128, first, last) == col).astype(BF16)
+        for y_ in range(NY):
+            c_, x_, dy_ = place(z * NY + y_)
+            ctp[:, y_ * 128 : (y_ + 1) * 128] = jnp.dot(
                 spread,
                 jnp.concatenate([part[c_, x_, dy_] for part in ct], axis=0),
                 preferred_element_type=F32,
             ).astype(BF16)
 
     def rs_copy(ch, d):
-        k = (zh + d) % 4
-        return pltpu.make_async_remote_copy(
-            src_ref=prb[ch].at[pl.ds(pl.multiple_of(k * 48, 16), 48), :], dst_ref=rsb[ch].at[d - 1],
+        return pltpu.make_async_remote_copy(
+            src_ref=prb[ch].at[(z + d) % NZ], dst_ref=rsb[ch].at[d - 1],
             send_sem=rss.at[ch, d - 1], recv_sem=rsr.at[ch, d - 1],
-            device_id=dev((z + 2 * d) % NZ, y, x, c), device_id_type=MESH,
+            device_id=dev((z + d) % NZ, y, x, c), device_id_type=MESH,
         )
 
     def ag_copy(ch, d, k):
-        part = pf[ch].at[pl.ds(pl.multiple_of(k * 48, 16), 48), :]
+        part = pf[ch].at[k]
         return pltpu.make_async_remote_copy(
             src_ref=part, dst_ref=part,
             send_sem=ags.at[ch, d - 1], recv_sem=agr.at[ch, d - 1],
-            device_id=dev((z + 2 * d) % NZ, y, x, c), device_id_type=MESH,
-        )
-
-    for ch in range(len(CHUNKS)):
-        for m in range(8):
-            pl.when(m != m_me)(lambda m=m: a2a_copy(ch, m, m).wait_recv())
-            pl.when(m == m_me)(lambda m=m: a2a_local(ch, m).wait())
+            device_id=dev((z + d) % NZ, y, x, c), device_id_type=MESH,
+        )
+
+    def pair(ch):
+        w = CHUNKS[ch][1]
+        q, full = w // 4, padded(w)
+        for m in range(NY):
+            pl.when(m != y)(lambda m=m: a2a_copy(ch, m, m).wait_recv())
+            pl.when(m == y)(lambda m=m: a2a_local(ch, m).wait())
         part = lax.dot_general(
-            ctp[...], hr[ch][...], (((1,), (1,)), ((), ())), preferred_element_type=F32
-        )
-        prf[ch][...] = part
-        prb[ch][...] = part.astype(BF16)
-        for d in range(1, 4):
+            hr[ch][...], ctp[...], (((1,), (1,)), ((), ())), preferred_element_type=F32
+        )
+        quarter = lax.broadcasted_iota(jnp.int32, (q, 128), 1) // 32
+        for k in range(NZ):
+            tail = jnp.zeros((q, 128), F32)
+            for i in range(4):
+                r0 = k * w + i * q
+                tail = jnp.where(quarter == i, part[r0 : r0 + q, 128:], tail)
+            rows = [part[k * w : (k + 1) * w, :128], tail]
+            if full > w + q:
+                rows.append(jnp.zeros((full - w - q, 128), F32))
+            rows = jnp.concatenate(rows, axis=0)
+            prf[ch][k] = rows
+            prb[ch][k] = rows.astype(BF16)
+        for d in around:
             send(functools.partial(rs_copy, ch, d))
 
-    finish()
-    mine = pl.ds(pl.multiple_of(zh * 48, 16), 48)
-    for ch in range(len(CHUNKS)):
-        for d in range(1, 4):
+    def reduce(ch):
+        for d in around:
             rs_copy(ch, d).wait_recv()
-        whole = prf[ch][mine, :]
-        for d in range(1, 4):
+        whole = prf[ch][z]
+        for d in around:
             whole = whole + rsb[ch][d - 1].astype(F32)
-        pf[ch][mine, :] = (whole * mscale).astype(BF16)
-        for d in range(1, 4):
-            send(functools.partial(ag_copy, ch, d, zh))
-
-    for ch in range(len(CHUNKS)):
-        for d in range(1, 4):
-            ag_copy(ch, d, (zh + 4 - d) % 4).wait_recv()
-        part = jnp.dot(pf[ch][...], hr[ch][...], preferred_element_type=F32)
+        pf[ch][z] = (whole * mscale).astype(BF16)
+        for d in around:
+            send(functools.partial(ag_copy, ch, d, z))
+
+    def apply(ch):
+        w = CHUNKS[ch][1]
+        q = w // 4
+        for d in around:
+            ag_copy(ch, d, (z + NZ - d) % NZ).wait_recv()
+        quarter = lax.broadcasted_iota(jnp.int32, (q, 128), 1) // 32
+        firsts, lasts = [], []
+        for k in range(NZ):
+            firsts.append(pf[ch][k, 0:w, :])
+            tail = pf[ch][k].astype(F32)[w : w + q]
+            for i in range(4):
+                lasts.append(jnp.where(quarter == i, tail, 0.0))
+        left = jnp.concatenate(
+            [jnp.concatenate(firsts, axis=0), jnp.concatenate(lasts, axis=0).astype(BF16)], axis=1
+        )
+        part = lax.dot_general(
+            left, hr[ch][...], (((0,), (0,)), ((), ())), preferred_element_type=F32
+        )
         if ch == 0:
             oacc[...] = part
         else:
             oacc[...] += part
 
+    steps = {"h": halves, "a": pair, "r": reduce, "g": apply}
+    for step in ORDER:
+        if step == "c":
+            group()
+        elif step == "f":
+            finish()
+        else:
+            steps[step[0]](int(step[1:]))
+
+    lasts = oacc[128:160, :] + oacc[160:192, :] + oacc[192:224, :] + oacc[224:256, :]
+    for c_ in range(NC):
+        fa[c_, 0:64, :] = oacc[c_ * 64 : (c_ + 1) * 64, :]
+        fa[c_, 64:80, :] = lasts[c_ * 16 : (c_ + 1) * 16]
     f1 = pltpu.make_async_remote_copy(
-        src_ref=oacc.at[pl.ds(pl.multiple_of((1 - c) * 96, 8), 96), :], dst_ref=frecv,
+        src_ref=fa.at[1 - c], dst_ref=frecv,
         send_sem=f1s, recv_sem=f1r, device_id=sibling, device_id_type=MESH,
     )
     send(lambda: f1)
     f1.wait_recv()
-    fsum[...] = oacc[pl.ds(pl.multiple_of(c * 96, 8), 96), :] + frecv[...]
-
+    fsum = fa[c] + frecv[...]
     for x_ in range(NX):
-        rows = [fsum[x_ * 24 : (x_ + 1) * 24, :], jnp.zeros((8, 1024), F32)]
-        fb[x_] = jnp.concatenate(rows, axis=0).astype(BF16)
+        rows = [
+            fsum[x_ * 16 : (x_ + 1) * 16],
+            fsum[64 + x_ * 4 : 64 + (x_ + 1) * 4],
+            jnp.zeros((12, NY * 128), F32),
+        ]
+        rows = jnp.concatenate(rows, axis=0)
+        fb[x_] = rows.astype(BF16)
+        ff[x_] = rows
 
     def f2_copy(i):
-        dx, dy, dl = rel[i]
-        x_, y_, l_ = (x + dx) % NX, (y + dy) % NY, (zl + dl) % 2
-        return pltpu.make_async_remote_copy(
-            src_ref=fb.at[x_, :, pl.ds(pl.multiple_of((y_ * 2 + l_) * 128, 128), 128)],
+        dx, dy = rel[i]
+        x_, y_ = (x + dx) % NX, (y + dy) % NY
+        return pltpu.make_async_remote_copy(
+            src_ref=fb.at[x_, :, pl.ds(pl.multiple_of(y_ * 128, 128), 128)],
             dst_ref=f2.at[i], send_sem=f2s.at[i], recv_sem=f2r.at[i],
-            device_id=rel_dev(dx, dy, dl), device_id_type=MESH,
+            device_id=rel_dev(dx, dy), device_id_type=MESH,
         )
 
     for i in reversed(range(len(rel))):
         send(functools.partial(f2_copy, i))
     finish()
-    done = fsum[
-        pl.ds(pl.multiple_of(x * 24, 8), 24), pl.ds(pl.multiple_of(m_me * 128, 128), 128)
-    ]
+    done = ff[x, :, pl.ds(pl.multiple_of(y * 128, 128), 128)]
     for i in range(len(rel)):
         f2_copy(i).wait_recv()
-        done = done + f2[i].astype(F32)[:24]
+        done = done + f2[i].astype(F32)
     o_ref[...] = (done * oscale)[:20, :bs]
+
+
+def padded(w):
+    return (w + w // 4 + 15) // 16 * 16
 
 
 def shards(three_centre, coeffs, neighbours, counts):
@@ -310,30 +364,31 @@
         pltpu.VMEM((nlist * 128, width), BF16),
         pltpu.VMEM((occ, 128), BF16),
         [pltpu.VMEM((NC, NX, NY, w, 128), BF16) for w in ws],
-        pltpu.VMEM((192, 1024), BF16),
+        pltpu.VMEM((256, NY * 128), BF16),
         [pltpu.VMEM((w, nlist * 128), BF16) for w in ws],
         [pltpu.VMEM((w, width), BF16) for w in ws],
-        [pltpu.VMEM((8, 4 * w, 128), BF16) for w in ws],
-        [pltpu.VMEM((4 * w, 1024), BF16) for w in ws],
-        [pltpu.VMEM((192, 4 * w), F32) for w in ws],
-        [pltpu.VMEM((192, 4 * w), BF16) for w in ws],
-        [pltpu.VMEM((3, 48, 4 * w), BF16) for w in ws],
-        [pltpu.VMEM((192, 4 * w), BF16) for w in ws],
-        pltpu.VMEM((192, 1024), F32),
-        pltpu.VMEM((96, 1024), F32),
-        pltpu.VMEM((96, 1024), F32),
-        pltpu.VMEM((NX, 32, 1024), BF16),
-        pltpu.VMEM((31, 32, 128), BF16),
+        [pltpu.VMEM((NY, NZ * w, 128), BF16) for w in ws],
+        [pltpu.VMEM((NZ * w, NY * 128), BF16) for w in ws],
+        [pltpu.VMEM((NZ, padded(w), 128), F32) for w in ws],
+        [pltpu.VMEM((NZ, padded(w), 128), BF16) for w in ws],
+        [pltpu.VMEM((NZ - 1, padded(w), 128), BF16) for w in ws],
+        [pltpu.VMEM((NZ, padded(w), 128), BF16) for w in ws],
+        pltpu.VMEM((256, NY * 128), F32),
+        pltpu.VMEM((NC, 80, NY * 128), F32),
+        pltpu.VMEM((80, NY * 128), F32),
+        pltpu.VMEM((NX, 32, NY * 128), BF16),
+        pltpu.VMEM((NX, 32, NY * 128), F32),
+        pltpu.VMEM((15, 32, 128), BF16),
         dma((nlist,)),
         dma((3,)),
         dma((n, NY)), dma((n, NY)),
         dma((n, 3)), dma((n, 3)),
         dma((n,)), dma((n,)),
-        dma((n, 8)), dma((n, 8)),
-        dma((n, 3)), dma((n, 3)),
-        dma((n, 3)), dma((n, 3)),
+        dma((n, NY)), dma((n, NY)),
+        dma((n, NZ - 1)), dma((n, NZ - 1)),
+        dma((n, NZ - 1)), dma((n, NZ - 1)),
         dma, dma,
-        dma((31,)), dma((31,)),
+        dma((15,)), dma((15,)),
     ]
     return pl.pallas_call(
         kernel,

time: 66.1 us -> 63.6 us (0.962)
  Pallas kernels: 64 us -> 61.4 us
    pallas_call x1, Pallas kernels: 64 us -> 61.4 us  [shards(): pl.pallas_call(kernel, out_shape=jax.ShapeDtypeStruct((occ // (NX * NC),...]
where the time goes in v3:
time: 63.6 us; the launch traced here: 63.4 us
  Pallas kernels  61.4 us (97%)
  local copies, waits for them, and re-layouts  1.31 us (2%)
  between operations  0.66 us (1%)
    pallas_call x1, Pallas kernels, shards(): pl.pallas_call(kernel, out_shape=jax.ShapeDtypeStruct((occ // (NX * NC),...  61.4 us
    unnamed x1, local copies, waits for them, and re-layouts  1.31 us

profile of v3, /device:TPU:1, one launch (start us, length us, event | category | flops | bytes accessed | tf_op | source)
XLA Modules:
  0.0 63.4 jit_solution(10100250495304731053)
XLA Ops:
  0.7 61.4 %shard_map.46 = f32[20,116]{1,0:T(8,128)} custom-call(bf16[1,7,116,3712]{3,2,1,0:T(8,128)(2,1)} %t_ref.1, bf16[160,116]{1,0:T(8,128)(2,1)} %bitcast.3, s32[1,7]{1,0:T(1,128)} %nbr_hbm.1, s32[1]{0:T(128)S(6)} %copy.6.cnt_hbm), custom_call_target="tpu_custom_call" | custom-call | tf_op jit(solution)/shard_map/pallas_call | solution.py:393
  62.1 1.3 %copy.7 = f32[116,20]{0,1:T(8,128)} copy(f32[116,20]{0,1:T(8,128)} %bitcast.2) | data formatting | bytes 18560

commit v4 on v3

--- a/solution.py
+++ b/solution.py
@@ -70,9 +70,6 @@
     cls = x * NC + c
     self_here = cls == 0
 
-    def s1_shift(dy):
-        return lax.rem(cls + 2 * dy, NZ)
-
     def rel_dev(dx, dy):
         return dev(z, (y + dy) % NY, (x + dx) % NX, c)
 
@@ -87,49 +84,39 @@
     hello(sibling)
     for d in around:
         hello(dev((z + d) % NZ, y, x, c))
-    for dy in range(NY):
-        source = dev((z + NZ - s1_shift(dy)) % NZ, (y + NY - dy) % NY, x, c)
-        if dy == 0:
-            pl.when(jnp.logical_not(self_here))(functools.partial(hello, source))
-        else:
-            hello(source)
 
     for load in small:
         load.wait()
     own[...] = jnp.concatenate([c_ref[...], jnp.zeros((occ, 128 - bs), BF16)], axis=1)
 
-    count = len(rel) + 1 + len(around) + NY
-    pl.semaphore_wait(barrier, jnp.where(self_here, count - 1, count))
-
-    def s1_copy(ch, dy):
+    pl.semaphore_wait(barrier, len(rel) + 1 + len(around))
+
+    def s1_copy(ch):
         r0, w = CHUNKS[ch]
         return pltpu.make_async_remote_copy(
-            src_ref=own.at[pl.ds(r0, w), :], dst_ref=ct[ch].at[c, x, dy],
-            send_sem=s1s.at[ch, dy], recv_sem=s1r.at[ch, dy],
-            device_id=dev((z + s1_shift(dy)) % NZ, (y + dy) % NY, x, c), device_id_type=MESH,
+            src_ref=own.at[pl.ds(r0, w), :], dst_ref=ct[ch].at[c, x, 0],
+            send_sem=s1s.at[ch], recv_sem=s1r.at[ch],
+            device_id=dev((z + cls) % NZ, y, x, c), device_id_type=MESH,
         )
 
     def s1_local(ch):
         r0, w = CHUNKS[ch]
-        return pltpu.make_async_copy(own.at[pl.ds(r0, w), :], ct[ch].at[c, x, 0], s1r.at[ch, 0])
+        return pltpu.make_async_copy(own.at[pl.ds(r0, w), :], ct[ch].at[c, x, 0], s1r.at[ch])
 
     for ch in range(len(CHUNKS)):
-        for dy in (2, 1, 3):
-            send(functools.partial(s1_copy, ch, dy))
-        send(functools.partial(s1_copy, ch, 0), jnp.logical_not(self_here))
+        send(functools.partial(s1_copy, ch), jnp.logical_not(self_here))
         pl.when(self_here)(lambda ch=ch: s1_local(ch).start())
 
     def s1_wait(ch):
-        for dy in range(1, NY):
-            s1_copy(ch, dy).wait_recv()
-        pl.when(jnp.logical_not(self_here))(lambda: s1_copy(ch, 0).wait_recv())
+        pl.when(jnp.logical_not(self_here))(lambda: s1_copy(ch).wait_recv())
         pl.when(self_here)(lambda: s1_local(ch).wait())
 
-    def s2_copy(ch, d, x_src):
-        part = ct[ch].at[c, x_src]
-        return pltpu.make_async_remote_copy(
-            src_ref=part, dst_ref=part, send_sem=s2s.at[ch, d - 1], recv_sem=s2r.at[ch, d - 1],
-            device_id=dev(z, y, (x + d) % NX, c), device_id_type=MESH,
+    def s2_copy(ch, i, x_src):
+        dx, dy = rel[i]
+        return pltpu.make_async_remote_copy(
+            src_ref=ct[ch].at[c, x, 0], dst_ref=ct[ch].at[c, x_src, dy],
+            send_sem=s2s.at[ch, i], recv_sem=s2r.at[ch, i],
+            device_id=rel_dev(dx, dy), device_id_type=MESH,
         )
 
     def core_copy(ch, c_src):
@@ -150,14 +137,13 @@
 
     for ch in range(len(CHUNKS)):
         s1_wait(ch)
-        for d in (2, 1, 3):
-            send(functools.partial(s2_copy, ch, d, x))
+        for i in reversed(range(len(rel))):
+            send(functools.partial(s2_copy, ch, i, x))
 
     def place(b):
         zb, yb = b // NY, b % NY
-        dy = (y + NY - yb) % NY
-        s = (z + 2 * NZ - zb - 2 * dy) % NZ
-        return s % NC, s // NC, dy
+        s = (z + NZ - zb) % NZ
+        return s % NC, s // NC, (y + NY - yb) % NY
 
     def a2a_copy(ch, to, source):
         lanes = pl.ds(pl.multiple_of(source * 128, 128), 128)
@@ -172,8 +158,8 @@
         return pltpu.make_async_copy(hs[ch].at[m], hr[ch].at[:, lanes], a2r.at[ch, m])
 
     def to_sibling(ch):
-        for d in range(1, NX):
-            s2_copy(ch, d, (x + NX - d) % NX).wait_recv()
+        for i in range(len(rel)):
+            s2_copy(ch, i, (x + NX - rel[i][0]) % NX).wait_recv()
         send(functools.partial(core_copy, ch, c))
 
     def halves(ch):
@@ -381,8 +367,8 @@
         pltpu.VMEM((15, 32, 128), BF16),
         dma((nlist,)),
         dma((3,)),
-        dma((n, NY)), dma((n, NY)),
-        dma((n, 3)), dma((n, 3)),
+        dma((n,)), dma((n,)),
+        dma((n, 15)), dma((n, 15)),
         dma((n,)), dma((n,)),
         dma((n, NY)), dma((n, NY)),
         dma((n, NZ - 1)), dma((n, NZ - 1)),

time: 63.6 us -> 63.4 us (level)
  no operation moved by 1% of the time
where the time goes in v4:
time: 63.4 us; the launch traced here: 63.2 us
  Pallas kernels  61.3 us (97%)
  local copies, waits for them, and re-layouts  1.31 us (2%)
  between operations  0.66 us (1%)
    pallas_call x1, Pallas kernels, shards(): pl.pallas_call(kernel, out_shape=jax.ShapeDtypeStruct((occ // (NX * NC),...  61.3 us
    unnamed x1, local copies, waits for them, and re-layouts  1.31 us

profile of v4, /device:TPU:1, one launch (start us, length us, event | category | flops | bytes accessed | tf_op | source)
XLA Modules:
  0.0 63.2 jit_solution(3250141809552759648)
XLA Ops:
  0.7 61.3 %shard_map.46 = f32[20,116]{1,0:T(8,128)} custom-call(bf16[1,7,116,3712]{3,2,1,0:T(8,128)(2,1)} %t_ref.1, bf16[160,116]{1,0:T(8,128)(2,1)} %bitcast.3, s32[1,7]{1,0:T(1,128)} %nbr_hbm.1, s32[1]{0:T(128)S(6)} %copy.6.cnt_hbm), custom_call_target="tpu_custom_call" | custom-call | tf_op jit(solution)/shard_map/pallas_call | solution.py:379
  61.9 1.3 %copy.7 = f32[116,20]{0,1:T(8,128)} copy(f32[116,20]{0,1:T(8,128)} %bitcast.2) | data formatting | bytes 18560
